TPU v7x, 32 devices: a whole 2x2x4 slice. The times are simulated.
32 devices in a mesh: outer: 2 (over x), member: 16 (over z, y, core).
Axes of the slice: x: 2, y: 2, z: 4, core: 2. Of those that a mesh axis runs over, the one named last changes fastest.
Arguments:
- vectors: bfloat16 [4096, 1024], P(('outer', 'member')), may hold values from -64 to 64
- list_ids: int32 [4096], P(('outer', 'member')), may hold values from 0 to 32767, as said below
- coarse_centroids: bfloat16 [32768, 1024], P('member'), may hold values from -3 to 3
- codebook: bfloat16 [16, 64, 2048], P('outer'), may hold values from -2 to 6
Outputs:
- reconstructed: bfloat16 [4096, 1024], P(('outer', 'member'))
- codebook_grad: float32 [16, 64, 2048], P('outer')
Inputs may be any that keep to these rules, and one draw needn't show every extreme that they name: `list_ids`: member j owns lists j * 2048 to (j + 1) * 2048 - 1. The 128 vectors of one device (an aligned block of the array) name lists of at most 16 vectors owned by any one member; in every pod one member owns the lists of exactly 16 vectors of every device of that pod.
All inputs are finite; a program needn't handle non-finite values.
Results may differ from a plain program's by a relative error of at most 0.0077.
Values may be sent and summed in bfloat16 or wider, within the bound.
A program may use at most 128 MiB of HBM per device.

v0:
```python
import jax
import jax.numpy as jnp
from jax import lax
from jax.sharding import PartitionSpec as P

logit_scale = 0.5


def quantize(residual, keep_row, codebook):
    n_subspace, sub_width, n_codes = codebook.shape
    row_count = residual.shape[0]
    block_rows = 256
    code_norm = jnp.sum(jnp.square(codebook.astype(jnp.float32)), axis=1)

    def one_block(running, block_input):
        row_piece, keep_piece = block_input
        split_rows = row_piece.reshape(block_rows, n_subspace, sub_width)
        products = jnp.einsum(
            "bsd,sdk->bsk", split_rows, codebook, preferred_element_type=jnp.float32
        )
        logits = logit_scale * (2.0 * products - code_norm[None])
        weights_low = jax.nn.softmax(logits, axis=-1).astype(jnp.bfloat16)
        rebuilt = jnp.einsum(
            "bsk,sdk->bsd", weights_low, codebook, preferred_element_type=jnp.float32
        )
        rebuilt = rebuilt.astype(jnp.bfloat16).reshape(block_rows, n_subspace * sub_width)
        kept_weights = weights_low * keep_piece[:, None, None]
        code_sums = running[0] + jnp.einsum(
            "bsd,bsk->sdk", split_rows, kept_weights, preferred_element_type=jnp.float32
        )
        counts = running[1] + jnp.sum(kept_weights.astype(jnp.float32), axis=0)
        return ((code_sums, counts), rebuilt)

    start = (
        jnp.zeros((n_subspace, sub_width, n_codes), jnp.float32),
        jnp.zeros((n_subspace, n_codes), jnp.float32),
    )
    blocks_in = (
        residual.reshape(-1, block_rows, residual.shape[1]),
        keep_row.reshape(-1, block_rows),
    )
    (code_sums, counts), rebuilt = lax.scan(one_block, start, blocks_in)
    return (rebuilt.reshape(row_count, residual.shape[1]), code_sums, counts)


def on_device(vectors, list_ids, coarse_centroids, codebook):
    rows_dev = vectors.shape[0]
    row_width = vectors.shape[1]
    members = lax.axis_size("member")
    outers = lax.axis_size("outer")
    lists_dev = coarse_centroids.shape[0]
    capacity = 2 * rows_dev // members
    owner_of = list_ids // lists_dev
    local_list = list_ids - owner_of * lists_dev
    onehot = (owner_of[:, None] == jnp.arange(members, dtype=jnp.int32)[None, :]).astype(jnp.int32)
    slot_rank = jnp.sum((jnp.cumsum(onehot, axis=0) - 1) * onehot, axis=1)
    slot_ids = jnp.full((members, capacity), -1, jnp.int32).at[owner_of, slot_rank].set(local_list)
    send_rows = (
        jnp.zeros((members, capacity, row_width), jnp.bfloat16).at[owner_of, slot_rank].set(vectors)
    )
    got_rows, got_ids = (
        lax.all_to_all(send_rows, "member", split_axis=0, concat_axis=0, tiled=True),
        lax.all_to_all(slot_ids, "member", split_axis=0, concat_axis=0, tiled=True),
    )
    flat_ids = got_ids.reshape(-1)
    valid_slot = flat_ids >= 0
    found_rows = jnp.take(coarse_centroids, jnp.maximum(flat_ids, 0), axis=0)
    difference = got_rows.reshape(-1, row_width).astype(jnp.float32) - found_rows.astype(
        jnp.float32
    )
    residual = jnp.where(valid_slot[:, None], difference, 0.0).astype(jnp.bfloat16)
    mark_cols = jnp.broadcast_to(valid_slot.astype(jnp.int32)[:, None], (flat_ids.shape[0], outers))
    sub_parts, flag_cols = (
        lax.all_to_all(residual, "outer", split_axis=1, concat_axis=0, tiled=True),
        lax.all_to_all(mark_cols, "outer", split_axis=1, concat_axis=0, tiled=True),
    )
    rebuilt, code_sums, counts = quantize(sub_parts, flag_cols[:, 0].astype(jnp.bfloat16), codebook)
    back_rows = lax.all_to_all(rebuilt, "outer", split_axis=0, concat_axis=1, tiled=True)
    full_rows = (found_rows.astype(jnp.float32) + back_rows.astype(jnp.float32)).astype(
        jnp.bfloat16
    )
    returned = lax.all_to_all(
        full_rows.reshape(members, capacity, row_width),
        "member",
        split_axis=0,
        concat_axis=0,
        tiled=True,
    )
    result = returned[owner_of, slot_rank]
    code_sums, counts = lax.psum((code_sums, counts), "member")
    vector_total = rows_dev * members * outers
    gradient = (
        2.0
        * codebook.shape[2]
        / vector_total
        * (counts[:, None, :] * codebook.astype(jnp.float32) - code_sums)
    )
    return (result, gradient)


def solution(mesh):
    return jax.shard_map(
        on_device,
        mesh=mesh,
        in_specs=(
            P(("outer", "member"), None),
            P(("outer", "member")),
            P("member", None),
            P("outer", None, None),
        ),
        out_specs=(P(("outer", "member"), None), P("outer", None, None)),
        check_vma=False,
    )
```

profile of v0, /device:TPU:0, one launch (start us, length us, event | category | flops | bytes accessed | tf_op | source)
XLA Modules:
  0.0 292.4 jit_solution(18361786958651140824)
XLA Ops:
  7.2 0.7 multiply_subtract_fusion
  7.8 0.1 fusion.19
  7.9 0.2 reduce_window_sum.11
  8.1 0.2 select_reduce_fusion
  8.3 0.6 broadcast_in_dim.67
  8.9 18.3 %scatter_fusion = s32[16,16]{1,0:T(8,128)} fusion(s32[16,16]{1,0:T(8,128)} %broadcast_in_dim.67, s32[128]{0:T(128)S(1)} %get-tuple-element.127, s32[128]{0:T(128)S(1)} %get-tuple-element.120), kind=kCustom, calls=%fused_computation.2 | custom fusion | bytes 2560 | tf_op jit(solution)/shard_map/scatter | solution.py:57
  27.2 7.3 %all-to-all-start = ((s32[16,1,16]{2,1,0:T(1,128)}), s32[16,1,16]{2,1,0:T(1,128)S(1)}, u32[]{:S(2)}, u32[]{:S(2)}) async-start(s32[16,1,16]{2,1,0:T(1,128)} %bitcast.4), calls=%async_computation | async-start | bytes 16384 | tf_op jit(solution)/shard_map/all_to_all | solution.py:63
  34.4 0.9 broadcast_in_dim.75
  35.3 18.9 %scatter_fusion.1 = bf16[16,16,1024]{2,1,0:T(8,128)(2,1)} fusion(bf16[16,16,1024]{2,1,0:T(8,128)(2,1)} %broadcast_in_dim.75, s32[128]{0:T(128)S(1)} %get-tuple-element.127, bf16[128,1024]{1,0:T(8,128)(2,1)} %param.6), kind=kCustom, calls=%fused_computation.3 | custom fusion | bytes 787456 | tf_op jit(solution)/shard_map/scatter | solution.py:59
  54.2 0.0 all-to-all-done
  54.2 6.0 %all-to-all-start.1 = ((bf16[16,16,1024]{2,1,0:T(8,128)(2,1)}), bf16[16,16,1024]{2,1,0:T(8,128)(2,1)S(1)}, u32[]{:S(2)}, u32[]{:S(2)}) async-start(bf16[16,16,1024]{2,1,0:T(8,128)(2,1)} %scatter_fusion.1), calls=%async_computation.1 | async-start | bytes 1048576 | tf_op jit(solution)/shard_map/all_to_all | solution.py:62
  60.2 0.1 ge.21
  60.3 0.1 le.21
  60.4 0.1 reshape.124
  60.5 4.3 %gather_fusion = bf16[256,1024]{1,0:T(8,128)(2,1)S(1)} fusion(bf16[2048,1024]{1,0:T(8,128)(2,1)} %param.8, s32[1024]{0:T(1024)S(1)} %pad_clamp_fusion), kind=kCustom, calls=%fused_computation | custom fusion | bytes 1049600 | tf_op jit(solution)/shard_map/jit(_take)/gather | solution.py:67
  64.8 0.0 copy-start.2
  64.8 0.0 copy-start.1
  64.8 1.2 gather.13
  66.0 8.7 %all-to-all-done.1 = bf16[16,16,1024]{2,1,0:T(8,128)(2,1)S(1)} async-done(((bf16[16,16,1024]{2,1,0:T(8,128)(2,1)}), bf16[16,16,1024]{2,1,0:T(8,128)(2,1)S(1)}, u32[]{:S(2)}, u32[]{:S(2)}) %all-to-all-start.1) | async-done | bytes 524320 | tf_op jit(solution)/shard_map/all_to_all | solution.py:62
  74.7 0.6 broadcast_in_dim.79
  75.2 3.2 %all-to-all-start.3 = ((s32[256,2,1]{0,2,1:T(1,128)}), s32[256,2,1]{0,2,1:T(1,128)S(1)}, u32[]{:S(2)}, u32[]{:S(2)}) async-start(s32[256,2,1]{0,2,1:T(1,128)} %broadcast_in_dim.79), calls=%async_computation.3 | async-start | bytes 4096 | tf_op jit(solution)/shard_map/all_to_all | solution.py:75
  78.5 1.9 reshape.120
  80.4 3.1 %select_convert_fusion = bf16[256,2,512]{2,1,0:T(2,128)(2,1)S(1)} fusion(f32[256,2,512]{2,1,0:T(2,128)} %reshape.120, pred[256]{0:T(512)(128)(4,1)S(1)} %ge.21, bf16[256,2,512]{2,1,0:T(2,128)(2,1)} %gather.13, pred[256]{0:T(512)(128)(4,1)S(1)} %le.21), kind=kLoop, calls=%fused_computation.33 | loop fusion | flops 1310720 | bytes 2097664 | tf_op jit(solution)/shard_map/convert_element_type | solution.py:71
  83.5 0.8 copy.17
  84.4 0.0 all-to-all-done.3
  84.4 3.5 %all-to-all-start.2 = ((bf16[256,2,512]{2,0,1:T(8,128)(2,1)}), bf16[256,2,512]{2,0,1:T(8,128)(2,1)S(1)}, u32[]{:S(2)}, u32[]{:S(2)}) async-start(bf16[256,2,512]{2,0,1:T(8,128)(2,1)} %copy.17), calls=%async_computation.2 | async-start | bytes 1048576 | tf_op jit(solution)/shard_map/all_to_all | solution.py:74
  87.9 0.2 all-reduce.3.cloned.1.call-start
  88.1 0.0 copy-done.1
  88.1 0.5 fusion.17
  88.6 0.0 copy-done.2
  88.7 7.6 %all-to-all-done.2 = bf16[256,2,512]{2,0,1:T(8,128)(2,1)S(1)} async-done(((bf16[256,2,512]{2,0,1:T(8,128)(2,1)}), bf16[256,2,512]{2,0,1:T(8,128)(2,1)S(1)}, u32[]{:S(2)}, u32[]{:S(2)}) %all-to-all-start.2) | async-done | bytes 524320 | tf_op jit(solution)/shard_map/all_to_all | solution.py:74
  96.3 61.6 %while.15 = (s32[]{:T(128)}, f32[8,64,2048]{2,1,0:T(8,128)}, f32[8,2048]{1,0:T(8,128)S(1)}, bf16[2,256,512]{1,2,0:T(8,128)(2,1)}, bf16[2,256,512]{2,1,0:T(8,128)...) while((s32[]{:T(128)}, f32[8,64,2048]{2,1,0:T(8,128)}, ...), condition=%wide.region_9.10_spmd.clone, body=%wide.region_5.9_spmd.clone.sunk | while | flops 1658996736 | bytes 111757520 | solution.py:42
  96.3 0.1 copy.25
  96.4 9.0 %fusion.45 = (f32[256,8]{0,1:T(8,128)S(1)}, f32[256,8,2048]{2,0,1:T(8,128)}) fusion(f32[8,2048]{1,0:T(8,128)S(1)} %get-tuple-element.211, bf16[256,8,64]{0,2,1:T(8,128)(2,1)S(1)} %bitcast.85, bf16[8,64,2048]{2,1,0:T(8,128)(2,1)S(1)} %get-tuple-element.210), kind=kOutput, calls=%fused_computation.58.clone.1 | convolution fusion | flops 557844480 | bytes 19210240 | tf_op jit(solution)/shard_map/while/body/eval_jaxpr/sub | solution.py:22
  105.4 10.2 %convert_reduce_fusion.2 = (f32[8,2048]{1,0:T(8,128)S(1)}, bf16[256,8,2048]{2,0,1:T(8,128)(2,1)}) fusion(bf16[256]{0:T(256)(128)(2,1)S(1)} %dynamic-slice_reduce_fusion.2, f32[256,8,2048]{2,0,1:T(8,128)} %get-tuple-element.181, f32[256,8]{0,1:T(8,128)S(1)} %get-tuple-element.182), kind=kLoop, calls=%fused_computation.9.clone.1 | loop fusion | flops 20955136 | bytes 25240064 | tf_op jit(solution)/shard_map/while/body/eval_jaxpr/reduce_sum | solution.py:31
  115.6 7.3 %select_add_fusion.4 = f32[8,64,2048]{2,1,0:T(8,128)} fusion(f32[8,64,2048]{2,1,0:T(8,128)} %get-tuple-element.196, bf16[256,8,64]{0,2,1:T(8,128)(2,1)S(1)} %bitcast.86, bf16[256,8,2048]{2,0,1:T(8,128)(2,1)} %get-tuple-element.183, bf16[256]{0:T(256)(128)(2,1)S(1)} %dynamic-slice_reduce_fusion.2, pred[]{:T(512)S(6)} %compare.19), kind=kOutput, calls=%fused_computation.17.clone.1 | convolution fusion | flops 543162368 | bytes 17039872 | tf_op jit(solution)/shard_map/while/body/eval_jaxpr/bsd,bsk->sdk/dot_general | solution.py:28
  122.9 0.0 copy-done
  122.9 2.7 convolution_convert_fusion.2
  125.6 0.0 copy-done.5
  125.6 0.0 copy-start.6
  125.6 0.9 copy-done.6
  126.5 0.1 copy.25
  126.7 9.0 %fusion.45 = (f32[256,8]{0,1:T(8,128)S(1)}, f32[256,8,2048]{2,0,1:T(8,128)}) fusion(f32[8,2048]{1,0:T(8,128)S(1)} %get-tuple-element.211, bf16[256,8,64]{0,2,1:T(8,128)(2,1)S(1)} %bitcast.85, bf16[8,64,2048]{2,1,0:T(8,128)(2,1)S(1)} %get-tuple-element.210), kind=kOutput, calls=%fused_computation.58.clone.1 | convolution fusion | flops 557844480 | bytes 19210240 | tf_op jit(solution)/shard_map/while/body/eval_jaxpr/sub | solution.py:22
  135.7 10.2 %convert_reduce_fusion.2 = (f32[8,2048]{1,0:T(8,128)S(1)}, bf16[256,8,2048]{2,0,1:T(8,128)(2,1)}) fusion(bf16[256]{0:T(256)(128)(2,1)S(1)} %dynamic-slice_reduce_fusion.2, f32[256,8,2048]{2,0,1:T(8,128)} %get-tuple-element.181, f32[256,8]{0,1:T(8,128)S(1)} %get-tuple-element.182), kind=kLoop, calls=%fused_computation.9.clone.1 | loop fusion | flops 20955136 | bytes 25240064 | tf_op jit(solution)/shard_map/while/body/eval_jaxpr/reduce_sum | solution.py:31
  145.9 8.5 %select_add_fusion.4 = f32[8,64,2048]{2,1,0:T(8,128)} fusion(f32[8,64,2048]{2,1,0:T(8,128)} %get-tuple-element.196, bf16[256,8,64]{0,2,1:T(8,128)(2,1)S(1)} %bitcast.86, bf16[256,8,2048]{2,0,1:T(8,128)(2,1)} %get-tuple-element.183, bf16[256]{0:T(256)(128)(2,1)S(1)} %dynamic-slice_reduce_fusion.2, pred[]{:T(512)S(6)} %compare.19), kind=kOutput, calls=%fused_computation.17.clone.1 | convolution fusion | flops 543162368 | bytes 17039872 | tf_op jit(solution)/shard_map/while/body/eval_jaxpr/bsd,bsk->sdk/dot_general | solution.py:28
  154.3 0.0 copy-done
  154.3 2.7 convolution_convert_fusion.2
  157.0 0.0 copy-done.5
  157.0 0.0 copy-start.6
  157.0 0.9 copy-done.6
  157.9 0.0 copy-start.4
  157.9 0.0 copy-start.7
  157.9 0.6 copy-done.4
  158.5 0.0 all-reduce.3.cloned.1.call-update
  158.6 0.4 copy-done.7
  159.0 10.0 %all_to_all.52 = bf16[2,256,512]{1,2,0:T(8,128)(2,1)S(1)} all-to-all(bf16[2,256,512]{1,2,0:T(8,128)(2,1)S(1)} %copy-done.7), channel_id=1, replica_groups=mesh['outer'=2,'member'=16] {'outer'}, dimensions={0} | all-to-all | bytes 1048576 | tf_op jit(solution)/shard_map/all_to_all | solution.py:78
  169.0 1.1 convert_bitcast_fusion
  170.1 2.3 copy.19
  172.4 3.2 %reshape.121 = f32[16,16,1024]{2,1,0:T(8,128)} reshape(f32[256,2,512]{2,1,0:T(2,128)} %copy.19) | data formatting | bytes 2097152 | tf_op jit(solution)/shard_map/convert_element_type | solution.py:79
  175.5 1.4 add_convert_fusion
  177.0 26.3 %all_to_all.53 = bf16[16,16,1024]{2,1,0:T(8,128)(2,1)S(1)} all-to-all(bf16[16,16,1024]{2,1,0:T(8,128)(2,1)S(1)} %add_convert_fusion), channel_id=1, replica_groups=mesh['outer'=2,'member'=16] {'member'}, dimensions={0} | all-to-all | bytes 1048576 | tf_op jit(solution)/shard_map/all_to_all | solution.py:82
  203.3 2.4 gather_fusion.1
  205.7 74.7 %all-reduce.3.cloned.1.call-done = (f32[8,64,2048]{2,1,0:T(8,128)}, f32[8,2048]{1,0:T(8,128)}) async-done(((f32[8,64,2048]{2,1,0:T(8,128)}, f32[8,2048]{1,0:T(8,128)}), (f32[8,64,2048]{2,1,0:T(8,128)}, f32[8,2048]{1,0:T(8,128)})) %all-reduce.3.cloned.1.call-update) | async-done | bytes 4259856 | tf_op jit(solution)/shard_map/psum | solution.py:90
  280.4 5.2 %fusion.18 = f32[8,64,2048]{2,1,0:T(8,128)} fusion(f32[8,64,2048]{2,1,0:T(8,128)} %get-tuple-element.116, bf16[8,64,2048]{2,1,0:T(8,128)(2,1)S(1)} %get-tuple-element.221, f32[8,2048]{1,0:T(8,128)} %get-tuple-element.117), kind=kLoop, calls=%fused_computation.30 | loop fusion | flops 3145728 | bytes 10551296 | tf_op jit(solution)/shard_map/sub | solution.py:96
  (24 shorter events, 0.2 us)
Async XLA Ops:
  27.2 27.0 %all-to-all-start = ((s32[16,1,16]{2,1,0:T(1,128)}), s32[16,1,16]{2,1,0:T(1,128)S(1)}, u32[]{:S(2)}, u32[]{:S(2)}) async-start(s32[16,1,16]{2,1,0:T(1,128)} %bitcast.4), calls=%async_computation | async-start | bytes 16384 | tf_op jit(solution)/shard_map/all_to_all | solution.py:63
  54.2 20.5 %all-to-all-start.1 = ((bf16[16,16,1024]{2,1,0:T(8,128)(2,1)}), bf16[16,16,1024]{2,1,0:T(8,128)(2,1)S(1)}, u32[]{:S(2)}, u32[]{:S(2)}) async-start(bf16[16,16,1024]{2,1,0:T(8,128)(2,1)} %scatter_fusion.1), calls=%async_computation.1 | async-start | bytes 1048576 | tf_op jit(solution)/shard_map/all_to_all | solution.py:62
  64.8 23.8 %copy-start.2 = (bf16[256,1024]{1,0:T(8,128)(2,1)}, bf16[256,1024]{1,0:T(8,128)(2,1)S(1)}, u32[]{:S(2)}) copy-start(bf16[256,1024]{1,0:T(8,128)(2,1)S(1)} %gather_fusion) | copy-start | bytes 1572868
  64.8 23.3 %copy-start.1 = (bf16[8,64,2048]{2,1,0:T(8,128)(2,1)S(1)}, bf16[8,64,2048]{2,1,0:T(8,128)(2,1)}, u32[]{:S(2)}) copy-start(bf16[8,64,2048]{2,1,0:T(8,128)(2,1)} %param.9) | copy-start | bytes 6291460
  75.2 9.1 %all-to-all-start.3 = ((s32[256,2,1]{0,2,1:T(1,128)}), s32[256,2,1]{0,2,1:T(1,128)S(1)}, u32[]{:S(2)}, u32[]{:S(2)}) async-start(s32[256,2,1]{0,2,1:T(1,128)} %broadcast_in_dim.79), calls=%async_computation.3 | async-start | bytes 4096 | tf_op jit(solution)/shard_map/all_to_all | solution.py:75
  84.4 11.9 %all-to-all-start.2 = ((bf16[256,2,512]{2,0,1:T(8,128)(2,1)}), bf16[256,2,512]{2,0,1:T(8,128)(2,1)S(1)}, u32[]{:S(2)}, u32[]{:S(2)}) async-start(bf16[256,2,512]{2,0,1:T(8,128)(2,1)} %copy.17), calls=%async_computation.2 | async-start | bytes 1048576 | tf_op jit(solution)/shard_map/all_to_all | solution.py:74
  87.9 192.5 %all-reduce.3.cloned.1.call-start = ((), (), s32[]{:S(2)}) async-start(), calls=%async_computation.6 | async-start | bytes 8519680 | tf_op jit(solution)/shard_map/psum | solution.py:90
  115.6 7.3 %copy-start = (bf16[256,8,2048]{2,0,1:T(8,128)(2,1)S(1)}, bf16[256,8,2048]{2,0,1:T(8,128)(2,1)}, u32[]{:S(2)}) copy-start(bf16[256,8,2048]{2,0,1:T(8,128)(2,1)} %get-tuple-element.183) | copy-start | bytes 25165828 | tf_op jit(solution)/shard_map/while
  122.9 2.7 copy-start.5
  125.6 0.9 copy-start.6
  145.9 8.5 %copy-start = (bf16[256,8,2048]{2,0,1:T(8,128)(2,1)S(1)}, bf16[256,8,2048]{2,0,1:T(8,128)(2,1)}, u32[]{:S(2)}) copy-start(bf16[256,8,2048]{2,0,1:T(8,128)(2,1)} %get-tuple-element.183) | copy-start | bytes 25165828 | tf_op jit(solution)/shard_map/while
  154.3 2.7 copy-start.5
  157.0 0.9 copy-start.6
  157.9 0.6 copy-start.4
  157.9 1.1 copy-start.7
  158.6 17.0 %copy-start.3 = (bf16[256,1024]{1,0:T(8,128)(2,1)S(1)}, bf16[256,1024]{1,0:T(8,128)(2,1)}, u32[]{:S(2)}) copy-start(bf16[256,1024]{1,0:T(8,128)(2,1)} %copy-done.2) | copy-start | bytes 1572868
Sparse Core Ops, SparseCore 0:
  158.7 121.6 all-reduce.2
where the time goes:
time: 294 us; the launch traced here: 292 us
  waiting for transfers between devices  91 us (31%)
  local copies, waits for them, and re-layouts  58.6 us (20%)
  matrix products  39 us (13%)
  blocking collectives  36.3 us (12%)
  other arithmetic  32.9 us (11%)
  starting transfers between devices  20.2 us (7%)
  between operations  14.2 us (5%)
    psum x1, waiting for transfers between devices, on_device(): code_sums, counts = lax.psum((code_sums, counts), 'member')  74.7 us
    all_to_all x1, blocking collectives, on_device(): lax.all_to_all(full_rows.reshape(members, capacity, row_width), 'member',...  26.3 us
    reduce_sum x2, other arithmetic, one_block(): counts = running[1] + jnp.sum(kept_weights.astype(jnp.float32), axis=0)  20.3 us
    scatter x1, local copies, waits for them, and re-layouts, on_device(): jnp.zeros((members, capacity, row_width), jnp.bfloat16)  18.9 us
    scatter x1, local copies, waits for them, and re-layouts, on_device(): jnp.full((members, capacity), -1, jnp.int32).at[owner_of, slot_rank]  18.3 us
    sub x2, matrix products, one_block(): weights_low = jax.nn.softmax(logits, axis=-1).astype(jnp.bfloat16)  18 us
    dot_general x2, matrix products, one_block(): jnp.einsum('bsd,bsk->sdk', split_rows, kept_weights, preferred_element_ty...  15.7 us
    all_to_all x1, blocking collectives, on_device(): lax.all_to_all(rebuilt, 'outer', split_axis=0, concat_axis=1, tiled=True)  9.99 us
  transfers between devices with their start and end apart: 5, of which 3 were waited for; matrix products, arithmetic and copies ran while one was open for 14% of the time, Pallas kernels for 0%

commit v1 on v0

v1 whole, which is shorter than its diff:
```python
import functools
import math

import jax
import jax.numpy as jnp
from jax import lax
from jax.experimental import pallas as pl
from jax.experimental.pallas import tpu as pltpu
from jax.sharding import PartitionSpec as P

LOG2E = math.log2(math.e)
F32, BF16 = jnp.float32, jnp.bfloat16


def pieces(x):
    hi = x.astype(BF16)
    rest = x - hi.astype(F32)
    mid = rest.astype(BF16)
    low = (rest - mid.astype(F32)).astype(BF16)
    return hi, mid, low


def one_subspace(code, res_t, scale):
    rows = res_t.shape[1]
    codes = code.shape[1]
    code_wide = code.astype(F32)
    norm = (-0.5 * LOG2E) * jnp.sum(code_wide * code_wide, axis=0, keepdims=True)
    hi, mid, low = pieces(norm)
    row_index = lax.broadcasted_iota(jnp.int32, (16, codes), 0)
    tail = jnp.where(
        row_index == 0,
        hi.astype(F32),
        jnp.where(row_index == 1, mid.astype(F32), jnp.where(row_index == 2, low.astype(F32), 0.0)),
    ).astype(BF16)
    right = jnp.concatenate([code, code, code, tail], axis=0)
    ones = jnp.ones((16, rows), BF16)
    left = jnp.concatenate([*pieces(res_t.astype(F32) * LOG2E), ones], axis=0)
    logits = lax.dot_general(left, right, (((0,), (0,)), ((), ())), preferred_element_type=F32)
    top = jnp.max(logits, axis=1, keepdims=True)
    raised = jnp.exp2(logits - top)
    total = jnp.sum(raised, axis=1, keepdims=True)
    weights = (raised * (1.0 / total)).astype(BF16)
    rebuilt_t = lax.dot_general(code, weights, (((1,), (1,)), ((), ())), preferred_element_type=F32)
    sums = jnp.dot(jnp.concatenate([res_t, ones], axis=0), weights, preferred_element_type=F32)
    sub = code.shape[0]
    counts = sums[sub : sub + 1, :]
    return rebuilt_t, scale * (counts * code_wide - sums[:sub, :])


def quantize_kernel(scale, sub, res_ref, cent_ref, code_ref, out_ref, grad_ref, res_t, reb_t):
    spaces = code_ref.shape[0]
    res_t[...] = res_ref[...].astype(F32).T.astype(BF16)

    @pl.loop(0, spaces)
    def _(space):
        at = pl.ds(pl.multiple_of(space * sub, sub), sub)
        rebuilt_t, grad = one_subspace(code_ref[space], res_t[at, :], scale)
        reb_t[at, :] = rebuilt_t
        grad_ref[space] = grad.astype(BF16)

    rebuilt = reb_t[...].T.astype(BF16).astype(F32)
    out_ref[...] = (cent_ref[...].astype(F32) + rebuilt).astype(BF16)


def quantize(scale, residual, cent, codebook):
    rows, cols = residual.shape
    spaces, sub, codes = codebook.shape
    vmem = pl.BlockSpec(memory_space=pltpu.VMEM)
    return pl.pallas_call(
        functools.partial(quantize_kernel, scale, sub),
        out_shape=(
            jax.ShapeDtypeStruct((rows, cols), BF16),
            jax.ShapeDtypeStruct((spaces, sub, codes), BF16),
        ),
        in_specs=[vmem] * 3,
        out_specs=(vmem, vmem),
        scratch_shapes=[pltpu.VMEM((cols, rows), BF16), pltpu.VMEM((cols, rows), F32)],
        compiler_params=pltpu.CompilerParams(vmem_limit_bytes=48 * 2**20),
    )(residual, cent, codebook)


def on_device(vectors, list_ids, coarse_centroids, codebook):
    rows_dev, row_width = vectors.shape
    members = lax.axis_size("member")
    outers = lax.axis_size("outer")
    lists_dev = coarse_centroids.shape[0]
    capacity = 2 * rows_dev // members
    cols = row_width // outers
    me = lax.axis_index("member")
    outer = lax.axis_index("outer")
    pair_rows = lax.all_to_all(vectors, "outer", split_axis=1, concat_axis=0, tiled=True)
    ids_all = lax.all_gather(list_ids, ("member", "outer"), axis=0, tiled=False)
    ids_all = ids_all.reshape(members * outers, rows_dev)
    ids_pair = lax.dynamic_slice_in_dim(ids_all, me * outers, outers, 0)
    before = jnp.triu(jnp.ones((rows_dev, rows_dev), BF16), 1)

    local = ids_all - me * lists_dev
    own = (local >= 0) & (local < lists_dev)
    rank = jnp.dot(own.astype(BF16), before, preferred_element_type=F32).astype(jnp.int32)
    slot = jnp.arange(capacity, dtype=jnp.int32)
    picked = own[:, None, :] & (rank[:, None, :] == slot[None, :, None])
    index = jnp.sum(jnp.where(picked, local[:, None, :], 0), axis=2).reshape(-1)
    onehot = (index[:, None] == jnp.arange(lists_dev, dtype=jnp.int32)[None, :]).astype(BF16)
    table = lax.dynamic_slice_in_dim(coarse_centroids, outer * cols, cols, 1)
    sent = jnp.dot(onehot, table, preferred_element_type=BF16)
    sent = sent.reshape(members, outers * capacity, cols)
    got = lax.all_to_all(sent, "member", split_axis=0, concat_axis=0, tiled=True)
    got = got.reshape(members, outers, capacity, cols)

    owner = ids_pair // lists_dev
    owned = owner[:, :, None] == jnp.arange(members, dtype=jnp.int32)
    count = jnp.einsum("nm,onj->omj", before, owned.astype(BF16), preferred_element_type=F32)
    rank = count.astype(jnp.int32)
    place = owned[:, :, :, None] & (rank[:, :, :, None] == slot)
    cent = jnp.einsum("onjr,jord->ond", place.astype(BF16), got, preferred_element_type=BF16)
    cent = cent.reshape(outers * rows_dev, cols)
    residual = (pair_rows.astype(F32) - cent.astype(F32)).astype(BF16)

    scale = 2.0 * codebook.shape[2] / (rows_dev * members * outers)
    full, partial = quantize(scale, residual, cent, codebook)
    result = lax.all_to_all(full, "outer", split_axis=0, concat_axis=1, tiled=True)
    gradient = reduce_member(partial)
    return (result, gradient)


def reduce_member(partial):
    flat = partial.reshape(-1, partial.shape[2])
    mine = lax.psum_scatter(flat, "member", scatter_dimension=0, tiled=True)
    return lax.all_gather(mine, "member", axis=0, tiled=True).reshape(partial.shape).astype(F32)


def solution(mesh):
    return jax.shard_map(
        on_device,
        mesh=mesh,
        in_specs=(
            P(("outer", "member"), None),
            P(("outer", "member")),
            P("member", None),
            P("outer", None, None),
        ),
        out_specs=(P(("outer", "member"), None), P("outer", None, None)),
        check_vma=False,
    )
```

time: 294 us -> 237 us (0.81)
  local copies, waits for them, and re-layouts: 58.6 us -> 2.85 us
  blocking collectives: 36.3 us -> 77.1 us
  matrix products: 39 us -> 4.38 us
  other arithmetic: 32.9 us -> 4.87 us
  waiting for transfers between devices: 91 us -> 114 us
  starting transfers between devices: 20.2 us -> 7.1 us
  Pallas kernels: 0 us -> 12.6 us
    psum x1 -> x0, waiting for transfers between devices: 74.7 us -> none  [on_device(): code_sums, counts = lax.psum((code_sums, counts), 'member')]
    all_gather x0 -> x1, blocking collectives: none -> 69.4 us  [on_device(): ids_all = lax.all_gather(list_ids, ('member', 'outer'), axis=0, tiled=False)]
    reduce_scatter x0 -> x1, waiting for transfers between devices: none -> 60.4 us  [reduce_member(): mine = lax.psum_scatter(flat, 'member', scatter_dimension=0, tiled=True)]
    scatter x2 -> x0, local copies, waits for them, and re-layouts: 37.1 us -> none  [the longest x1 18.9 us: on_device(): jnp.zeros((members, capacity, row_width), jnp.bfloat16)]
    all_gather x0 -> x1, waiting for transfers between devices: none -> 34.4 us  [reduce_member(): lax.all_gather(mine, 'member', axis=0, tiled=True).reshape(partial.shape)]
    all_to_all x2 -> x1, blocking collectives: 36.3 us -> 7.67 us  [on_device(): lax.all_to_all(full, 'outer', split_axis=0, concat_axis=1, tiled=True)]
    reduce_sum x4 -> x1, other arithmetic: 21 us -> 0.62 us  [on_device(): index = jnp.sum(jnp.where(picked, local[:, None, :], 0), axis=2).reshape(-1)]
    sub x2 -> x0, matrix products: 18 us -> none  [one_block(): weights_low = jax.nn.softmax(logits, axis=-1).astype(jnp.bfloat16)]
  transfers between devices with their start and end apart: 5 -> 4, of which waited for: 3 -> 4; matrix products, arithmetic and copies ran while one was open for 14% -> 1% of each run, Pallas kernels for 0% -> 0%
where the time goes in v1:
time: 237 us
  waiting for transfers between devices  114 us (48%)
  blocking collectives  77.1 us (33%)
  between operations  14.1 us (6%)
  Pallas kernels  12.6 us (5%)
  starting transfers between devices  7.1 us (3%)
  other arithmetic  4.87 us (2%)
  matrix products  4.38 us (2%)
  local copies, waits for them, and re-layouts  2.85 us (1%)
    all_gather x1, blocking collectives, on_device(): ids_all = lax.all_gather(list_ids, ('member', 'outer'), axis=0, tiled=False)  69.4 us
    reduce_scatter x1, waiting for transfers between devices, reduce_member(): mine = lax.psum_scatter(flat, 'member', scatter_dimension=0, tiled=True)  60.4 us
    all_gather x1, waiting for transfers between devices, reduce_member(): lax.all_gather(mine, 'member', axis=0, tiled=True).reshape(partial.shape)  34.4 us
    all_to_all x1, waiting for transfers between devices, on_device(): lax.all_to_all(sent, 'member', split_axis=0, concat_axis=0, tiled=True)  13.5 us
    pallas_call x1, Pallas kernels, quantize(): pl.pallas_call(functools.partial(quantize_kernel, scale, sub), out_shape=...  12.6 us
    all_to_all x1, blocking collectives, on_device(): lax.all_to_all(full, 'outer', split_axis=0, concat_axis=1, tiled=True)  7.67 us
    all_to_all x1, waiting for transfers between devices, on_device(): lax.all_to_all(vectors, 'outer', split_axis=1, concat_axis=0, tiled=True)  5.28 us
  transfers between devices with their start and end apart: 4, of which 4 were waited for; matrix products, arithmetic and copies ran while one was open for 1% of the time, Pallas kernels for 0%

profile of v1, /device:TPU:0, one launch (start us, length us, event | category | flops | bytes accessed | tf_op | source)
XLA Modules:
  0.0 236.7 jit_solution(8277067576626729066)
XLA Ops:
  7.2 69.4 %all-gather.1 = s32[32,1,128]{2,1,0:T(1,128)S(1)} all-gather(s32[1,1,128]{2,1,0:T(1,128)} %bitcast.47), channel_id=2, replica_groups=mesh['outer'=2,'member'=16] {'member','outer'}, dimensions={0}, use_global_device_ids=true | all-gather | bytes 16896 | tf_op jit(solution)/shard_map/all_gather | solution.py:92
  76.6 0.1 convolution_convert_fusion
  76.8 0.6 select_reduce_fusion
  77.4 0.1 eq.67
  77.5 0.0 copy-start.2
  77.5 0.0 copy-start
  77.5 3.8 %fusion = bf16[512,512]{1,0:T(8,128)(2,1)} fusion(bf16[2048,1024]{1,0:T(8,128)(2,1)} %param.6, s32[]{:T(128)S(6)} %select_n.25, s32[512]{0:T(512)S(1)} %eq.67), kind=kOutput, calls=%fused_computation.1 | convolution fusion | flops 1074790400 | bytes 2623492 | tf_op jit(solution)/shard_map/dot_general | solution.py:105
  81.3 3.6 %all-to-all-start.1 = ((bf16[16,32,512]{2,1,0:T(8,128)(2,1)}), bf16[16,32,512]{2,1,0:T(8,128)(2,1)S(1)}, u32[]{:S(2)}, u32[]{:S(2)}) async-start(bf16[16,32,512]{2,1,0:T(8,128)(2,1)} %bitcast.7), calls=%async_computation.1 | async-start | bytes 1048576 | tf_op jit(solution)/shard_map/all_to_all | solution.py:107
  84.9 0.0 copy-done.2
  84.9 0.7 copy.23
  85.7 0.1 fusion.3
  85.8 13.5 %all-to-all-done.1 = bf16[16,32,512]{2,1,0:T(8,128)(2,1)S(1)} async-done(((bf16[16,32,512]{2,1,0:T(8,128)(2,1)}), bf16[16,32,512]{2,1,0:T(8,128)(2,1)S(1)}, u32[]{:S(2)}, u32[]{:S(2)}) %all-to-all-start.1) | async-done | bytes 524320 | tf_op jit(solution)/shard_map/all_to_all | solution.py:107
  99.3 3.4 %all-to-all-start = ((bf16[128,2,512]{2,0,1:T(8,128)(2,1)}), bf16[128,2,512]{2,0,1:T(8,128)(2,1)S(1)}, u32[]{:S(2)}, u32[]{:S(2)}) async-start(bf16[128,2,512]{2,0,1:T(8,128)(2,1)} %bitcast.32), calls=%async_computation | async-start | bytes 524288 | tf_op jit(solution)/shard_map/all_to_all | solution.py:91
  102.8 0.0 reduce-scatter.2.cloned.1.call-start
  102.8 0.3 fusion.5
  103.1 5.3 %all-to-all-done = bf16[128,2,512]{2,0,1:T(8,128)(2,1)S(1)} async-done(((bf16[128,2,512]{2,0,1:T(8,128)(2,1)}), bf16[128,2,512]{2,0,1:T(8,128)(2,1)S(1)}, u32[]{:S(2)}, u32[]{:S(2)}) %all-to-all-start) | async-done | bytes 262176 | tf_op jit(solution)/shard_map/all_to_all | solution.py:91
  108.4 0.1 fusion.4.res_ref
  108.5 0.0 copy-done
  108.5 12.6 %shard_map.59 = (bf16[256,512]{1,0:T(8,128)(2,1)S(1)}, bf16[8,64,2048]{2,1,0:T(8,128)(2,1)S(1)}) custom-call(bf16[256,512]{1,0:T(8,128)(2,1)S(1)} %fusion.4.res_ref, bf16[256,512]{1,0:T(8,128)(2,1)S(1)} %bitcast.36, bf16[8,64,2048]{2,1,0:T(8,128)(2,1)S(1)} %copy-done), custom_call_target="tpu_custom_call" | custom-call | tf_op jit(solution)/shard_map/pallas_call | solution.py:69
  121.1 0.0 copy-start.1
  121.1 1.3 copy-done.1
  122.4 0.0 reduce-scatter.2.cloned.1.call-update
  122.5 0.0 all-gather.4.cloned.1.call-start
  122.5 60.4 %reduce-scatter.2.cloned.1.call-done = bf16[32,2048]{1,0:T(8,128)(2,1)} async-done(((bf16[512,2048]{1,0:T(8,128)(2,1)}), bf16[32,2048]{1,0:T(8,128)(2,1)}) %reduce-scatter.2.cloned.1.call-update) | async-done | bytes 131088 | tf_op jit(solution)/shard_map/reduce_scatter | solution.py:128
  182.9 0.0 all-gather.4.cloned.1.call-update
  183.0 7.7 %all_to_all.37 = bf16[2,128,512]{2,1,0:T(8,128)(2,1)S(1)} all-to-all(bf16[2,128,512]{2,1,0:T(8,128)(2,1)S(1)} %bitcast.37), channel_id=1, replica_groups=mesh['outer'=2,'member'=16] {'outer'}, dimensions={0} | all-to-all | bytes 524288 | tf_op jit(solution)/shard_map/all_to_all | solution.py:121
  190.6 0.7 copy.19
  191.4 34.4 %all-gather.4.cloned.1.call-done = bf16[512,2048]{1,0:T(8,128)(2,1)} async-done(((bf16[32,2048]{1,0:T(8,128)(2,1)}), bf16[512,2048]{1,0:T(8,128)(2,1)}) %all-gather.4.cloned.1.call-update) | async-done | bytes 2097168 | tf_op jit(solution)/shard_map/all_gather | solution.py:129
  225.7 4.1 %convert.3 = f32[8,64,2048]{2,1,0:T(8,128)} convert(bf16[8,64,2048]{2,1,0:T(8,128)(2,1)} %bitcast.38) | non-fusion elementwise | flops 1048576 | bytes 6291456 | tf_op jit(solution)/shard_map/convert_element_type | solution.py:129
  (5 shorter events, 0.0 us)
Async XLA Ops:
  77.5 7.4 %copy-start.2 = (bf16[128,1024]{1,0:T(8,128)(2,1)S(1)}, bf16[128,1024]{1,0:T(8,128)(2,1)}, u32[]{:S(2)}) copy-start(bf16[128,1024]{1,0:T(8,128)(2,1)} %param.4) | copy-start | bytes 786436
  77.5 31.0 %copy-start = (bf16[8,64,2048]{2,1,0:T(8,128)(2,1)S(1)}, bf16[8,64,2048]{2,1,0:T(8,128)(2,1)}, u32[]{:S(2)}) copy-start(bf16[8,64,2048]{2,1,0:T(8,128)(2,1)} %code_ref.1) | copy-start | bytes 6291460
  81.3 18.0 %all-to-all-start.1 = ((bf16[16,32,512]{2,1,0:T(8,128)(2,1)}), bf16[16,32,512]{2,1,0:T(8,128)(2,1)S(1)}, u32[]{:S(2)}, u32[]{:S(2)}) async-start(bf16[16,32,512]{2,1,0:T(8,128)(2,1)} %bitcast.7), calls=%async_computation.1 | async-start | bytes 1048576 | tf_op jit(solution)/shard_map/all_to_all | solution.py:107
  99.3 9.1 %all-to-all-start = ((bf16[128,2,512]{2,0,1:T(8,128)(2,1)}), bf16[128,2,512]{2,0,1:T(8,128)(2,1)S(1)}, u32[]{:S(2)}, u32[]{:S(2)}) async-start(bf16[128,2,512]{2,0,1:T(8,128)(2,1)} %bitcast.32), calls=%async_computation | async-start | bytes 524288 | tf_op jit(solution)/shard_map/all_to_all | solution.py:91
  102.8 80.2 %reduce-scatter.2.cloned.1.call-start = ((), (), s32[]{:S(2)}) async-start(), calls=%async_computation.4 | async-start | bytes 2228224 | tf_op jit(solution)/shard_map/reduce_scatter | solution.py:128
  121.1 1.3 copy-start.1
  122.5 103.3 %all-gather.4.cloned.1.call-start = ((), (), s32[]{:S(2)}) async-start(), calls=%async_computation.5 | async-start | bytes 2228224 | tf_op jit(solution)/shard_map/all_gather | solution.py:129
Sparse Core Ops, SparseCore 0:
  122.6 60.2 reduce-scatter.1
  185.3 40.3 all-gather.3

commit v2 on v1

v2 whole, which is shorter than its diff:
```python
import functools
import math

import jax
import jax.numpy as jnp
from jax import lax
from jax.experimental import pallas as pl
from jax.experimental.pallas import tpu as pltpu
from jax.sharding import PartitionSpec as P

MESH = pl.DeviceIdType.MESH
LOG2E = math.log2(math.e)
F32, BF16 = jnp.float32, jnp.bfloat16


def pieces(x):
    hi = x.astype(BF16)
    rest = x - hi.astype(F32)
    mid = rest.astype(BF16)
    low = (rest - mid.astype(F32)).astype(BF16)
    return hi, mid, low


def one_subspace(code, res_t, scale):
    rows = res_t.shape[1]
    codes = code.shape[1]
    code_wide = code.astype(F32)
    norm = (-0.5 * LOG2E) * jnp.sum(code_wide * code_wide, axis=0, keepdims=True)
    hi, mid, low = pieces(norm)
    row_index = lax.broadcasted_iota(jnp.int32, (16, codes), 0)
    tail = jnp.where(
        row_index == 0,
        hi.astype(F32),
        jnp.where(row_index == 1, mid.astype(F32), jnp.where(row_index == 2, low.astype(F32), 0.0)),
    ).astype(BF16)
    right = jnp.concatenate([code, code, code, tail], axis=0)
    ones = jnp.ones((16, rows), BF16)
    left = jnp.concatenate([*pieces(res_t.astype(F32) * LOG2E), ones], axis=0)
    logits = lax.dot_general(left, right, (((0,), (0,)), ((), ())), preferred_element_type=F32)
    top = jnp.max(logits, axis=1, keepdims=True)
    raised = jnp.exp2(logits - top)
    total = jnp.sum(raised, axis=1, keepdims=True)
    weights = (raised * (1.0 / total)).astype(BF16)
    rebuilt_t = lax.dot_general(code, weights, (((1,), (1,)), ((), ())), preferred_element_type=F32)
    sums = jnp.dot(jnp.concatenate([res_t, ones], axis=0), weights, preferred_element_type=F32)
    sub = code.shape[0]
    counts = sums[sub : sub + 1, :]
    return rebuilt_t, scale * (counts * code_wide - sums[:sub, :])


def later_on(axis, step):
    size = lax.axis_size(axis)
    return lax.rem(lax.axis_index(axis) + step, size)


def greet(axis_targets):
    barrier = pltpu.get_barrier_semaphore()
    for target in axis_targets:
        pl.semaphore_signal(barrier, inc=1, device_id=target, device_id_type=MESH)
    return barrier


def fetch_kernel(
    capacity,
    ids_ref,
    vec_ref,
    table_hbm,
    res_ref,
    cent_ref,
    table,
    ids_pair,
    ids_all,
    vec_got,
    sent,
    got,
    table_sem,
    pair_send,
    pair_recv,
    vec_send,
    vec_recv,
    ids_send,
    ids_recv,
    row_send,
    row_recv,
):
    members, outers = lax.axis_size("member"), lax.axis_size("outer")
    me, outer = lax.axis_index("member"), lax.axis_index("outer")
    lists_dev, cols = table.shape
    rows_dev = vec_ref.shape[0]
    block = outers * capacity
    slots = members * block

    def part(index):
        return pl.ds(pl.multiple_of(index * cols, cols), cols)

    def block_of(index):
        return pl.ds(pl.multiple_of(index * block, block), block)

    table_copy = pltpu.make_async_copy(table_hbm.at[:, part(outer)], table, table_sem)
    table_copy.start()
    barrier = greet([{"outer": later_on("outer", step)} for step in range(1, outers)])

    @pl.loop(1, members)
    def _(step):
        pl.semaphore_signal(
            barrier, inc=1, device_id={"member": later_on("member", step)}, device_id_type=MESH
        )

    ids_pair[outer] = ids_ref[...]
    vec_got[outer] = vec_ref[:, part(outer)]
    pl.semaphore_wait(barrier, outers + members - 2)

    def outer_copies(step):
        target = later_on("outer", step)
        ids_copy = pltpu.make_async_remote_copy(
            src_ref=ids_ref,
            dst_ref=ids_pair.at[outer],
            send_sem=pair_send.at[step],
            recv_sem=pair_recv.at[step],
            device_id={"outer": target},
            device_id_type=MESH,
        )
        vec_copy = pltpu.make_async_remote_copy(
            src_ref=vec_ref.at[:, part(target)],
            dst_ref=vec_got.at[outer],
            send_sem=vec_send.at[step],
            recv_sem=vec_recv.at[step],
            device_id={"outer": target},
            device_id_type=MESH,
        )
        return ids_copy, vec_copy

    outer_pairs = [outer_copies(step) for step in range(1, outers)]
    for ids_copy, _ in outer_pairs:
        ids_copy.start()
    for ids_copy, _ in outer_pairs:
        ids_copy.wait()

    def ids_copy_of(step):
        return pltpu.make_async_remote_copy(
            src_ref=ids_pair,
            dst_ref=ids_all.at[me],
            send_sem=ids_send.at[step],
            recv_sem=ids_recv.at[step],
            device_id={"member": later_on("member", step)},
            device_id_type=MESH,
        )

    @pl.loop(1, members)
    def _(step):
        ids_copy_of(step).start()

    for _, vec_copy in outer_pairs:
        vec_copy.start()

    ids_all[me] = ids_pair[...]
    row_index = lax.broadcasted_iota(jnp.int32, (rows_dev, rows_dev), 0)
    col_index = lax.broadcasted_iota(jnp.int32, (rows_dev, rows_dev), 1)
    before = jnp.where(row_index < col_index, 1.0, 0.0).astype(BF16)
    slot = lax.broadcasted_iota(jnp.int32, (slots, rows_dev), 0)
    slot_rank = lax.rem(slot, capacity).astype(F32)

    def picked(local):
        own = (local >= 0) & (local < lists_dev)
        rank = jnp.dot(jnp.where(own, 1.0, 0.0).astype(BF16), before, preferred_element_type=F32)
        return own & (rank == slot_rank)

    @pl.loop(1, members)
    def _(step):
        ids_copy_of(step).wait()

    ids = ids_all[...].reshape(members * outers, 1, rows_dev)
    ids = jnp.broadcast_to(ids, (members * outers, capacity, rows_dev)).reshape(slots, rows_dev)
    local = ids - me * lists_dev
    index = jnp.sum(jnp.where(picked(local), local.astype(F32), 0.0), axis=1, keepdims=True)
    lists = lax.broadcasted_iota(jnp.int32, (slots, lists_dev), 1)
    onehot = jnp.where(lists == index.astype(jnp.int32), 1.0, 0.0).astype(BF16)
    table_copy.wait()
    sent[...] = jnp.dot(onehot, table[...], preferred_element_type=F32).astype(BF16)

    def row_copy_of(step):
        target = later_on("member", step)
        return pltpu.make_async_remote_copy(
            src_ref=sent.at[block_of(target)],
            dst_ref=got.at[block_of(me)],
            send_sem=row_send.at[step],
            recv_sem=row_recv.at[step],
            device_id={"member": target},
            device_id_type=MESH,
        )

    @pl.loop(1, members)
    def _(step):
        row_copy_of(step).start()

    got[block_of(me)] = sent[block_of(me)]
    slot_owner = lax.div(slot, block)
    slot_outer = lax.rem(lax.div(slot, capacity), outers)
    places = []
    for source in range(outers):
        wanted = jnp.broadcast_to(ids_pair[source], (slots, rows_dev)) - slot_owner * lists_dev
        place = picked(wanted) & (slot_outer == source)
        places.append(jnp.where(place, 1.0, 0.0).T.astype(BF16))

    for _, vec_copy in outer_pairs:
        vec_copy.wait()

    @pl.loop(1, members)
    def _(step):
        row_copy_of(step).wait()

    for source in range(outers):
        cent = jnp.dot(places[source], got[...], preferred_element_type=F32)
        at = pl.ds(source * rows_dev, rows_dev)
        cent_ref[at, :] = cent.astype(BF16)
        res_ref[at, :] = (vec_got[source].astype(F32) - cent).astype(BF16)


def fetch(vectors, list_ids, coarse_centroids):
    rows_dev, row_width = vectors.shape
    members, outers = lax.axis_size("member"), lax.axis_size("outer")
    lists_dev = coarse_centroids.shape[0]
    capacity = max(2 * rows_dev // members, 16 // outers, 8)
    cols = row_width // outers
    slots = members * outers * capacity
    vmem = pl.BlockSpec(memory_space=pltpu.VMEM)
    dma = pltpu.SemaphoreType.DMA
    out = jax.ShapeDtypeStruct((outers * rows_dev, cols), BF16)
    return pl.pallas_call(
        functools.partial(fetch_kernel, capacity),
        out_shape=(out, out),
        in_specs=[vmem, vmem, pl.BlockSpec(memory_space=pl.ANY)],
        out_specs=(vmem, vmem),
        scratch_shapes=[
            pltpu.VMEM((lists_dev, cols), BF16),
            pltpu.VMEM((outers, 1, rows_dev), jnp.int32),
            pltpu.VMEM((members, outers, 1, rows_dev), jnp.int32),
            pltpu.VMEM((outers, rows_dev, cols), BF16),
            pltpu.VMEM((slots, cols), BF16),
            pltpu.VMEM((slots, cols), BF16),
            dma,
            *[dma((outers,))] * 4,
            *[dma((members,))] * 4,
        ],
        compiler_params=pltpu.CompilerParams(
            collective_id=0, has_side_effects=True, vmem_limit_bytes=48 * 2**20
        ),
    )(list_ids.reshape(1, rows_dev), vectors, coarse_centroids)


def halving_plan(members, height, width):
    plan = []
    for _ in range(members.bit_length() - 1):
        if height > 16:
            height //= 2
        else:
            width //= 2
        plan.append((height, width))
    return plan


def quantize_kernel(
    scale,
    sub,
    plan,
    res_ref,
    cent_ref,
    code_ref,
    out_ref,
    grad_ref,
    res_t,
    reb_t,
    back,
    acc,
    *rest,
):
    steps = len(plan)
    arriving, leaving = rest[:steps], rest[steps : 2 * steps]
    sum_send, sum_recv, gather_send, gather_recv, back_send, back_recv = rest[2 * steps :]
    groups, height, width = acc.shape
    per_group = height // sub
    rows_dev = out_ref.shape[0]
    outers = lax.axis_size("outer")
    me, outer = lax.axis_index("member"), lax.axis_index("outer")
    cols = res_ref.shape[1]

    bits = [lax.rem(lax.div(me, 2**step), 2) for step in range(steps)]
    partners = [me + (1 - 2 * bits[step]) * 2**step for step in range(steps)]
    barrier = greet(
        [{"outer": later_on("outer", step)} for step in range(1, outers)]
        + [{"member": partner} for partner in partners]
    )

    starts = [(0, 0)]
    for step, (high, wide) in enumerate(plan):
        row, col = starts[-1]
        was_high = height if step == 0 else plan[step - 1][0]
        if was_high != high:
            starts.append((row + bits[step] * high, col))
        else:
            starts.append((row, col + bits[step] * wide))

    def block(step, start):
        high, wide = plan[step]
        return (
            pl.ds(pl.multiple_of(start[0], 16), high),
            pl.ds(pl.multiple_of(start[1], 128), wide),
        )

    def kept(step):
        return block(step, starts[step + 1])

    def given(step):
        row, col = starts[step]
        kept_row, kept_col = starts[step + 1]
        high, wide = plan[step]
        was_high = height if step == 0 else plan[step - 1][0]
        if was_high != high:
            return block(step, (row + (1 - bits[step]) * high, col))
        return block(step, (row, col + (1 - bits[step]) * wide))

    def sum_copy(step, group):
        return pltpu.make_async_remote_copy(
            src_ref=leaving[step].at[group],
            dst_ref=arriving[step].at[group],
            send_sem=sum_send.at[step, group],
            recv_sem=sum_recv.at[step, group],
            device_id={"member": partners[step]},
            device_id_type=MESH,
        )

    def gather_copy(step, group):
        where = kept(step)
        return pltpu.make_async_remote_copy(
            src_ref=grad_ref.at[group, where[0], where[1]],
            dst_ref=grad_ref.at[group, where[0], where[1]],
            send_sem=gather_send.at[step, group],
            recv_sem=gather_recv.at[step, group],
            device_id={"member": partners[step]},
            device_id_type=MESH,
        )

    def send_sum(step, group):
        rows, columns = given(step)
        leaving[step][group] = acc[group, rows, columns].astype(BF16)
        sum_copy(step, group).start()

    def take_sum(step, group):
        sum_copy(step, group).wait()
        rows, columns = kept(step)
        total = acc[group, rows, columns] + arriving[step][group].astype(F32)
        if step + 1 < steps:
            acc[group, rows, columns] = total
            send_sum(step + 1, group)
        else:
            grad_ref[group, rows, columns] = total.astype(BF16)
            gather_copy(step, group).start()

    def take_gather(step, group):
        gather_copy(step, group).wait()
        if step > 0:
            gather_copy(step - 1, group).start()

    def advance(tick):
        for stage in range(2 * steps, 0, -1):
            group = tick - stage

            @pl.when((group >= 0) & (group < groups))
            def _(stage=stage, group=group):
                if stage <= steps:
                    take_sum(stage - 1, group)
                else:
                    take_gather(2 * steps - stage, group)

    res_t[...] = res_ref[...].astype(F32).T.astype(BF16)
    pl.semaphore_wait(barrier, outers - 1 + steps)

    @pl.loop(0, groups)
    def _(tick):
        for inner in range(per_group):
            space = tick * per_group + inner
            at = pl.ds(pl.multiple_of(space * sub, sub), sub)
            rebuilt_t, grad = one_subspace(code_ref[space], res_t[at, :], scale)
            reb_t[at, :] = rebuilt_t
            acc[tick, inner * sub : (inner + 1) * sub, :] = grad
        advance(tick)
        send_sum(0, tick)

    rebuilt = reb_t[...].T.astype(BF16).astype(F32)
    full = (cent_ref[...].astype(F32) + rebuilt).astype(BF16)
    for source in range(outers):
        back[source] = full[source * rows_dev : (source + 1) * rows_dev, :]
    here = pl.ds(pl.multiple_of(outer * cols, cols), cols)

    def back_copy(step):
        target = later_on("outer", step)
        return pltpu.make_async_remote_copy(
            src_ref=back.at[target],
            dst_ref=out_ref.at[:, here],
            send_sem=back_send.at[step],
            recv_sem=back_recv.at[step],
            device_id={"outer": target},
            device_id_type=MESH,
        )

    for step in range(1, outers):
        back_copy(step).start()
    out_ref[:, here] = back[outer]

    @pl.loop(groups, groups + 2 * steps)
    def _(tick):
        advance(tick)

    for step in range(1, outers):
        back_copy(step).wait()


def quantize(scale, residual, cent, codebook):
    rows, cols = residual.shape
    spaces, sub, codes = codebook.shape
    members, outers = lax.axis_size("member"), lax.axis_size("outer")
    per_group = 1
    while per_group * sub * codes // members < 16 * 128:
        per_group *= 2
    groups, height = spaces // per_group, per_group * sub
    plan = halving_plan(members, height, codes)
    vmem = pl.BlockSpec(memory_space=pltpu.VMEM)
    dma = pltpu.SemaphoreType.DMA
    pieces_moving = [pltpu.VMEM((groups, high, wide), BF16) for high, wide in plan]
    full, grad = pl.pallas_call(
        functools.partial(quantize_kernel, scale, sub, plan),
        out_shape=(
            jax.ShapeDtypeStruct((rows // outers, cols * outers), BF16),
            jax.ShapeDtypeStruct((groups, height, codes), BF16),
        ),
        in_specs=[vmem] * 3,
        out_specs=(vmem, vmem),
        scratch_shapes=[
            pltpu.VMEM((cols, rows), BF16),
            pltpu.VMEM((cols, rows), F32),
            pltpu.VMEM((outers, rows // outers, cols), BF16),
            pltpu.VMEM((groups, height, codes), F32),
            *pieces_moving,
            *pieces_moving,
            *[dma((len(plan), groups))] * 4,
            *[dma((outers,))] * 2,
        ],
        compiler_params=pltpu.CompilerParams(
            collective_id=1, has_side_effects=True, vmem_limit_bytes=48 * 2**20
        ),
    )(residual, cent, codebook)
    return full, grad.reshape(codebook.shape).astype(F32)


def on_device(vectors, list_ids, coarse_centroids, codebook):
    members, outers = lax.axis_size("member"), lax.axis_size("outer")
    residual, cent = fetch(vectors, list_ids, coarse_centroids)
    scale = 2.0 * codebook.shape[2] / (vectors.shape[0] * members * outers)
    return quantize(scale, residual, cent, codebook)


def solution(mesh):
    return jax.shard_map(
        on_device,
        mesh=mesh,
        in_specs=(
            P(("outer", "member"), None),
            P(("outer", "member")),
            P("member", None),
            P("outer", None, None),
        ),
        out_specs=(P(("outer", "member"), None), P("outer", None, None)),
        check_vma=False,
    )
```

time: 237 us -> 89.2 us (0.38)
  waiting for transfers between devices: 114 us -> 0 us
  blocking collectives: 77.1 us -> 0 us
  Pallas kernels: 12.6 us -> 81.3 us
  between operations: 14.1 us -> 0.67 us
  starting transfers between devices: 7.1 us -> 0 us
  matrix products: 4.38 us -> 0 us
    all_gather x1 -> x0, blocking collectives: 69.4 us -> none  [on_device(): ids_all = lax.all_gather(list_ids, ('member', 'outer'), axis=0, tiled=False)]
    pallas_call x1 -> x2, Pallas kernels: 12.6 us -> 81.3 us  [the longest x1 55.9 us: quantize(): pl.pallas_call(functools.partial(quantize_kernel, scale, sub, plan), out_...]
    reduce_scatter x1 -> x0, waiting for transfers between devices: 60.4 us -> none  [reduce_member(): mine = lax.psum_scatter(flat, 'member', scatter_dimension=0, tiled=True)]
    all_gather x1 -> x0, waiting for transfers between devices: 34.4 us -> none  [reduce_member(): lax.all_gather(mine, 'member', axis=0, tiled=True).reshape(partial.shape)]
    all_to_all x2 -> x0, waiting for transfers between devices: 18.8 us -> none  [the longest x1 13.5 us: on_device(): lax.all_to_all(sent, 'member', split_axis=0, concat_axis=0, tiled=True)]
    all_to_all x1 -> x0, blocking collectives: 7.67 us -> none  [on_device(): lax.all_to_all(full, 'outer', split_axis=0, concat_axis=1, tiled=True)]
    all_to_all x2 -> x0, starting transfers between devices: 7.02 us -> none  [the longest x1 3.57 us: on_device(): lax.all_to_all(sent, 'member', split_axis=0, concat_axis=0, tiled=True)]
    dot_general x4 -> x0, matrix products: 4.38 us -> none  [the longest x1 3.84 us: on_device(): sent = jnp.dot(onehot, table, preferred_element_type=BF16)]
  transfers between devices with their start and end apart: 4 -> 0, of which waited for: 4 -> 0; matrix products, arithmetic and copies ran while one was open for 1% -> 0% of each run, Pallas kernels for 0% -> 0%
where the time goes in v2:
time: 89.2 us; the launch traced here: 89 us
  Pallas kernels  81.3 us (91%)
  local copies, waits for them, and re-layouts  4.49 us (5%)
  other arithmetic  2.54 us (3%)
    pallas_call x1, Pallas kernels, quantize(): pl.pallas_call(functools.partial(quantize_kernel, scale, sub, plan), out_...  55.9 us
    pallas_call x1, Pallas kernels, fetch(): pl.pallas_call(functools.partial(fetch_kernel, capacity), out_shape=(out,...  25.4 us
    unnamed x9, local copies, waits for them, and re-layouts  4.49 us
    convert_element_type x1, other arithmetic, quantize(): return (full, grad.reshape(codebook.shape).astype(F32))  2.54 us

profile of v2, /device:TPU:0, one launch (start us, length us, event | category | flops | bytes accessed | tf_op | source)
XLA Modules:
  0.0 89.0 jit_solution(137995501147518573)
XLA Ops:
  0.6 0.0 copy-start
  0.6 2.2 %copy-done = bf16[2048,1024]{1,0:T(8,128)(2,1)S(1)} copy-done((bf16[2048,1024]{1,0:T(8,128)(2,1)S(1)}, bf16[2048,1024]{1,0:T(8,128)(2,1)}, u32[]{:S(2)}) %copy-start) | copy-done | bytes 4194328
  2.8 0.0 copy-start.2
  2.8 0.9 %copy-done.2 = bf16[128,1024]{1,0:T(8,128)(2,1)S(1)} copy-done((bf16[128,1024]{1,0:T(8,128)(2,1)S(1)}, bf16[128,1024]{1,0:T(8,128)(2,1)}, u32[]{:S(2)}) %copy-start.2) | copy-done | bytes 262168
  3.8 0.0 copy-start.3
  3.8 0.7 copy-done.3
  4.4 0.0 copy-start.1
  4.4 25.4 %shard_map.59 = (bf16[256,512]{1,0:T(8,128)(2,1)S(1)}, bf16[256,512]{1,0:T(8,128)(2,1)S(1)}) custom-call(s32[1,128]{1,0:T(1,128)S(1)} %bitcast.1, bf16[128,1024]{1,0:T(8,128)(2,1)S(1)} %copy-done.2, bf16[2048,1024]{1,0:T(8,128)(2,1)S(1)} %copy-done), custom_call_target="tpu_custom_call" | custom-call | tf_op jit(solution)/shard_map/pallas_call | solution.py:229
  29.9 0.0 copy-done.1
  29.9 55.9 %shard_map.60 = (bf16[128,1024]{1,0:T(8,128)(2,1)S(1)}, bf16[8,64,2048]{2,1,0:T(8,128)(2,1)S(1)}) custom-call(bf16[256,512]{1,0:T(8,128)(2,1)S(1)} %get-tuple-element.6.res_ref, bf16[256,512]{1,0:T(8,128)(2,1)S(1)} %get-tuple-element.7.cent_ref, bf16[8,64,2048]{2,1,0:T(8,128)(2,1)S(1)} %copy-done.1), custom_call_target="tpu_custom_call" | custom-call | tf_op jit(solution)/shard_map/pallas_call | solution.py:430
  85.8 2.5 %convert_element_type.3 = f32[8,64,2048]{2,1,0:T(8,128)} convert(bf16[8,64,2048]{2,1,0:T(8,128)(2,1)S(1)} %get-tuple-element.9) | non-fusion elementwise | flops 1048576 | bytes 6291456 | tf_op jit(solution)/shard_map/convert_element_type | solution.py:452
  88.3 0.7 copy.7
Async XLA Ops:
  0.6 2.2 %copy-start = (bf16[2048,1024]{1,0:T(8,128)(2,1)S(1)}, bf16[2048,1024]{1,0:T(8,128)(2,1)}, u32[]{:S(2)}) copy-start(bf16[2048,1024]{1,0:T(8,128)(2,1)} %table_hbm.1) | copy-start | bytes 12582916
  2.8 0.9 %copy-start.2 = (bf16[128,1024]{1,0:T(8,128)(2,1)S(1)}, bf16[128,1024]{1,0:T(8,128)(2,1)}, u32[]{:S(2)}) copy-start(bf16[128,1024]{1,0:T(8,128)(2,1)} %vec_ref.1) | copy-start | bytes 786436
  3.8 0.7 copy-start.3
  4.4 25.4 %copy-start.1 = (bf16[8,64,2048]{2,1,0:T(8,128)(2,1)S(1)}, bf16[8,64,2048]{2,1,0:T(8,128)(2,1)}, u32[]{:S(2)}) copy-start(bf16[8,64,2048]{2,1,0:T(8,128)(2,1)} %code_ref.1) | copy-start | bytes 6291460

commit v3 on v1

v3 whole, which is shorter than its diff:
```python
import functools
import math

import jax
import jax.numpy as jnp
from jax import lax
from jax.experimental import pallas as pl
from jax.experimental.pallas import tpu as pltpu
from jax.sharding import PartitionSpec as P

MESH = pl.DeviceIdType.MESH
LOG2E = math.log2(math.e)
F32, BF16 = jnp.float32, jnp.bfloat16


def pieces(x):
    hi = x.astype(BF16)
    rest = x - hi.astype(F32)
    mid = rest.astype(BF16)
    low = (rest - mid.astype(F32)).astype(BF16)
    return hi, mid, low


def one_subspace(code, res_t, scale):
    rows = res_t.shape[1]
    codes = code.shape[1]
    code_wide = code.astype(F32)
    norm = (-0.5 * LOG2E) * jnp.sum(code_wide * code_wide, axis=0, keepdims=True)
    hi, mid, low = pieces(norm)
    row_index = lax.broadcasted_iota(jnp.int32, (16, codes), 0)
    tail = jnp.where(
        row_index == 0,
        hi.astype(F32),
        jnp.where(row_index == 1, mid.astype(F32), jnp.where(row_index == 2, low.astype(F32), 0.0)),
    ).astype(BF16)
    right = jnp.concatenate([code, code, code, tail], axis=0)
    ones = jnp.ones((16, rows), BF16)
    left = jnp.concatenate([*pieces(res_t.astype(F32) * LOG2E), ones], axis=0)
    logits = lax.dot_general(left, right, (((0,), (0,)), ((), ())), preferred_element_type=F32)
    top = jnp.max(logits, axis=1, keepdims=True)
    raised = jnp.exp2(logits - top)
    total = jnp.sum(raised, axis=1, keepdims=True)
    weights = (raised * (1.0 / total)).astype(BF16)
    rebuilt_t = lax.dot_general(code, weights, (((1,), (1,)), ((), ())), preferred_element_type=F32)
    sums = jnp.dot(jnp.concatenate([res_t, ones], axis=0), weights, preferred_element_type=F32)
    sub = code.shape[0]
    counts = sums[sub : sub + 1, :]
    return rebuilt_t, scale * (counts * code_wide - sums[:sub, :])


def later_on(axis, step):
    size = lax.axis_size(axis)
    return lax.rem(lax.axis_index(axis) + step, size)


def greet(axis_targets):
    barrier = pltpu.get_barrier_semaphore()
    for target in axis_targets:
        pl.semaphore_signal(barrier, inc=1, device_id=target, device_id_type=MESH)
    return barrier


def split_plan(members, height, width):
    plan, stride = [], 1
    while stride < members:
        left = members // stride
        factor = 2 if stride < 4 or left == 2 else 4
        by_rows = height // factor >= 16
        if by_rows:
            height //= factor
        else:
            width //= factor
        plan.append((factor, stride, by_rows, height, width))
        stride *= factor
    return plan


def step_kernel(
    scale,
    sub,
    capacity,
    plan,
    ids_hbm,
    vec_hbm,
    table_hbm,
    code_hbm,
    out_ref,
    grad_ref,
    ids_own,
    vec_own,
    table,
    code_ref,
    ids_pair,
    ids_all,
    vec_got,
    sent,
    got,
    cent_ref,
    res_t,
    reb_t,
    back,
    acc,
    *rest,
):
    stages = len(plan)
    arriving, leaving = rest[:stages], rest[stages : 2 * stages]
    sum_send, sum_recv = rest[2 * stages : 3 * stages], rest[3 * stages : 4 * stages]
    gather_send, gather_recv = rest[4 * stages : 5 * stages], rest[5 * stages : 6 * stages]
    (
        load_sem,
        table_sem,
        pair_send,
        pair_recv,
        vec_send,
        vec_recv,
        back_send,
        back_recv,
        ids_send,
        ids_recv,
        row_send,
        row_recv,
    ) = rest[6 * stages :]
    members, outers = lax.axis_size("member"), lax.axis_size("outer")
    me, outer = lax.axis_index("member"), lax.axis_index("outer")
    parts, lists_dev, part_cols = table.shape
    cols = parts * part_cols
    rows_dev = vec_own.shape[0]
    block = outers * capacity
    slots = members * block
    groups, height, width = acc.shape
    per_group = height // sub

    def columns_of(index, size):
        return pl.ds(pl.multiple_of(index * size, size), size)

    def block_of(index):
        return pl.ds(pl.multiple_of(index * block, block), block)

    loads = [
        pltpu.make_async_copy(ids_hbm, ids_own, load_sem.at[0]),
        pltpu.make_async_copy(vec_hbm, vec_own, load_sem.at[1]),
        pltpu.make_async_copy(code_hbm, code_ref, load_sem.at[2]),
    ]
    table_copies = [
        pltpu.make_async_copy(
            table_hbm.at[:, columns_of(outer * parts + part, part_cols)],
            table.at[part],
            table_sem.at[part],
        )
        for part in range(parts)
    ]
    loads[0].start()
    loads[1].start()
    for copy in table_copies:
        copy.start()
    loads[2].start()
    barrier = greet([{"outer": later_on("outer", step)} for step in range(1, outers)])

    @pl.loop(1, members)
    def _(step):
        pl.semaphore_signal(
            barrier, inc=1, device_id={"member": later_on("member", step)}, device_id_type=MESH
        )

    loads[0].wait()
    ids_pair[outer] = ids_own[...]
    loads[1].wait()
    here = columns_of(outer, cols)
    vec_got[outer] = vec_own[:, here]
    pl.semaphore_wait(barrier, outers + members - 2)

    def outer_copies(step):
        target = later_on("outer", step)
        ids_copy = pltpu.make_async_remote_copy(
            src_ref=ids_own,
            dst_ref=ids_pair.at[outer],
            send_sem=pair_send.at[step],
            recv_sem=pair_recv.at[step],
            device_id={"outer": target},
            device_id_type=MESH,
        )
        vec_copy = pltpu.make_async_remote_copy(
            src_ref=vec_own.at[:, columns_of(target, cols)],
            dst_ref=vec_got.at[outer],
            send_sem=vec_send.at[step],
            recv_sem=vec_recv.at[step],
            device_id={"outer": target},
            device_id_type=MESH,
        )
        return ids_copy, vec_copy

    outer_pairs = [outer_copies(step) for step in range(1, outers)]
    for ids_copy, _ in outer_pairs:
        ids_copy.start()
    for ids_copy, _ in outer_pairs:
        ids_copy.wait()

    def ids_copy_of(step):
        return pltpu.make_async_remote_copy(
            src_ref=ids_pair,
            dst_ref=ids_all.at[me],
            send_sem=ids_send.at[step],
            recv_sem=ids_recv.at[step],
            device_id={"member": later_on("member", step)},
            device_id_type=MESH,
        )

    @pl.loop(1, members)
    def _(step):
        ids_copy_of(step).start()

    for _, vec_copy in outer_pairs:
        vec_copy.start()

    ids_all[me] = ids_pair[...]
    row_index = lax.broadcasted_iota(jnp.int32, (rows_dev, rows_dev), 0)
    col_index = lax.broadcasted_iota(jnp.int32, (rows_dev, rows_dev), 1)
    before = jnp.where(row_index < col_index, 1.0, 0.0).astype(BF16)
    slot = lax.broadcasted_iota(jnp.int32, (slots, rows_dev), 0)
    slot_rank = lax.rem(slot, capacity).astype(F32)

    def picked(local):
        own = (local >= 0) & (local < lists_dev)
        rank = jnp.dot(jnp.where(own, 1.0, 0.0).astype(BF16), before, preferred_element_type=F32)
        return own & (rank == slot_rank)

    slot_owner = lax.div(slot, block)
    slot_outer = lax.rem(lax.div(slot, capacity), outers)
    places = []
    for source in range(outers):
        wanted = jnp.broadcast_to(ids_pair[source], (slots, rows_dev)) - slot_owner * lists_dev
        place = picked(wanted) & (slot_outer == source)
        places.append(jnp.where(place, 1.0, 0.0).T.astype(BF16))
    place_all = jnp.concatenate(places, axis=0)

    @pl.loop(1, members)
    def _(step):
        ids_copy_of(step).wait()

    ids = ids_all[...].reshape(members * outers, 1, rows_dev)
    ids = jnp.broadcast_to(ids, (members * outers, capacity, rows_dev)).reshape(slots, rows_dev)
    local = ids - me * lists_dev
    index = jnp.sum(jnp.where(picked(local), local.astype(F32), 0.0), axis=1, keepdims=True)
    lists = lax.broadcasted_iota(jnp.int32, (slots, lists_dev), 1)
    onehot = jnp.where(lists == index.astype(jnp.int32), 1.0, 0.0).astype(BF16)

    def row_copy_of(part, step):
        target = later_on("member", step)
        return pltpu.make_async_remote_copy(
            src_ref=sent.at[part, block_of(target)],
            dst_ref=got.at[part, block_of(me)],
            send_sem=row_send.at[part, step],
            recv_sem=row_recv.at[part, step],
            device_id={"member": target},
            device_id_type=MESH,
        )

    for part in range(parts):
        table_copies[part].wait()
        sent[part] = jnp.dot(onehot, table[part], preferred_element_type=F32).astype(BF16)

        @pl.loop(1, members)
        def _(step, part=part):
            row_copy_of(part, step).start()

        got[part, block_of(me)] = sent[part, block_of(me)]

    digits = [lax.rem(lax.div(me, stride), factor) for factor, stride, *_ in plan]

    def partner(stage, step):
        factor, stride = plan[stage][:2]
        digit = digits[stage]
        return me + (lax.rem(digit + step, factor) - digit) * stride

    starts = [(0, 0)]
    for (factor, stride, by_rows, high, wide), digit in zip(plan, digits):
        row, col = starts[-1]
        starts.append((row + digit * high, col) if by_rows else (row, col + digit * wide))

    def place_of(stage, start):
        high, wide = plan[stage][3:]
        return (
            pl.ds(pl.multiple_of(start[0], 16), high),
            pl.ds(pl.multiple_of(start[1], 128), wide),
        )

    def kept(stage):
        return place_of(stage, starts[stage + 1])

    def given(stage, step):
        factor, _, by_rows, high, wide = plan[stage]
        row, col = starts[stage]
        digit = lax.rem(digits[stage] + step, factor)
        return place_of(stage, (row + digit * high, col) if by_rows else (row, col + digit * wide))

    def sum_copy(stage, group, step):
        return pltpu.make_async_remote_copy(
            src_ref=leaving[stage].at[group, step - 1],
            dst_ref=arriving[stage].at[group, step - 1],
            send_sem=sum_send[stage].at[group, step - 1],
            recv_sem=sum_recv[stage].at[group, step - 1],
            device_id={"member": partner(stage, step)},
            device_id_type=MESH,
        )

    def gather_copy(stage, group, step):
        rows, columns = kept(stage)
        return pltpu.make_async_remote_copy(
            src_ref=grad_ref.at[group, rows, columns],
            dst_ref=grad_ref.at[group, rows, columns],
            send_sem=gather_send[stage].at[group, step - 1],
            recv_sem=gather_recv[stage].at[group, step - 1],
            device_id={"member": partner(stage, step)},
            device_id_type=MESH,
        )

    def others(stage):
        return range(1, plan[stage][0])

    def send_sum(stage, group):
        for step in others(stage):
            rows, columns = given(stage, step)
            leaving[stage][group, step - 1] = acc[group, rows, columns].astype(BF16)
            sum_copy(stage, group, step).start()

    def send_gather(stage, group):
        for step in others(stage):
            gather_copy(stage, group, step).start()

    def take_sum(stage, group):
        for step in others(stage):
            sum_copy(stage, group, step).wait()
        rows, columns = kept(stage)
        total = acc[group, rows, columns]
        for step in others(stage):
            total = total + arriving[stage][group, step - 1].astype(F32)
        if stage + 1 < stages:
            acc[group, rows, columns] = total
            send_sum(stage + 1, group)
        else:
            grad_ref[group, rows, columns] = total.astype(BF16)
            send_gather(stage, group)

    def take_gather(stage, group):
        for step in others(stage):
            gather_copy(stage, group, step).wait()
        if stage > 0:
            send_gather(stage - 1, group)

    work = [(take_sum, stage) for stage in range(stages)]
    work += [(take_gather, stage) for stage in reversed(range(stages))]
    lags, lag = [], 0
    for _, stage in work:
        lag += 1 if stage == 0 else 2
        lags.append(lag)

    def advance(tick):
        for (take, stage), lag in reversed(list(zip(work, lags))):
            group = tick - lag

            @pl.when((group >= 0) & (group < groups))
            def _(take=take, stage=stage, group=group):
                take(stage, group)

    for _, vec_copy in outer_pairs:
        vec_copy.wait()
    loads[2].wait()
    part_groups = groups // parts

    @pl.loop(0, parts)
    def _(part):
        @pl.loop(1, members)
        def _(step):
            row_copy_of(part, step).wait()

        cent = jnp.dot(place_all, got[part], preferred_element_type=F32)
        cent_ref[part] = cent.astype(BF16)
        at = columns_of(part, part_cols)
        vec = jnp.concatenate([vec_got[source, :, at] for source in range(outers)], axis=0)
        residual = (vec.astype(F32) - cent).astype(BF16).astype(F32)
        res_t[at, :] = residual.T.astype(BF16)

        @pl.loop(0, part_groups)
        def _(inner_group):
            tick = part * part_groups + inner_group
            for inner in range(per_group):
                space = tick * per_group + inner
                at = pl.ds(pl.multiple_of(space * sub, sub), sub)
                rebuilt_t, grad = one_subspace(code_ref[space], res_t[at, :], scale)
                reb_t[at, :] = rebuilt_t
                acc[tick, inner * sub : (inner + 1) * sub, :] = grad
            advance(tick)
            send_sum(0, tick)

    rebuilt = reb_t[...].T.astype(BF16).astype(F32)
    for part in range(parts):
        at = slice(part * part_cols, (part + 1) * part_cols)
        full = (cent_ref[part].astype(F32) + rebuilt[:, at]).astype(BF16)
        for source in range(outers):
            back[source, :, at] = full[source * rows_dev : (source + 1) * rows_dev, :]

    def back_copy(step):
        target = later_on("outer", step)
        return pltpu.make_async_remote_copy(
            src_ref=back.at[target],
            dst_ref=out_ref.at[:, here],
            send_sem=back_send.at[step],
            recv_sem=back_recv.at[step],
            device_id={"outer": target},
            device_id_type=MESH,
        )

    for step in range(1, outers):
        back_copy(step).start()
    out_ref[:, here] = back[outer]

    @pl.loop(groups, groups + lags[-1])
    def _(tick):
        advance(tick)

    for step in range(1, outers):
        back_copy(step).wait()


PARTS = 2


def on_device(vectors, list_ids, coarse_centroids, codebook):
    rows_dev, row_width = vectors.shape
    members, outers = lax.axis_size("member"), lax.axis_size("outer")
    lists_dev = coarse_centroids.shape[0]
    capacity = max(2 * rows_dev // members, 16 // outers, 8)
    cols = row_width // outers
    slots = members * outers * capacity
    rows = outers * rows_dev
    spaces, sub, codes = codebook.shape
    scale = 2.0 * codes / (rows_dev * members * outers)
    per_group = 1
    while per_group * sub * codes // members < 16 * 128:
        per_group *= 2
    groups, height = spaces // per_group, per_group * sub
    parts = min(PARTS, groups, cols // 128)
    part_cols = cols // parts
    plan = split_plan(members, height, codes)
    vmem = pl.BlockSpec(memory_space=pltpu.VMEM)
    anywhere = pl.BlockSpec(memory_space=pl.ANY)
    dma = pltpu.SemaphoreType.DMA
    moving = [pltpu.VMEM((groups, item[0] - 1, item[3], item[4]), BF16) for item in plan]
    moving_sems = [dma((groups, item[0] - 1)) for item in plan]
    full, grad = pl.pallas_call(
        functools.partial(step_kernel, scale, sub, capacity, plan),
        out_shape=(
            jax.ShapeDtypeStruct((rows_dev, row_width), BF16),
            jax.ShapeDtypeStruct((groups, height, codes), BF16),
        ),
        in_specs=[anywhere] * 4,
        out_specs=(vmem, vmem),
        scratch_shapes=[
            pltpu.VMEM((1, rows_dev), jnp.int32),
            pltpu.VMEM((rows_dev, row_width), BF16),
            pltpu.VMEM((parts, lists_dev, part_cols), BF16),
            pltpu.VMEM(codebook.shape, BF16),
            pltpu.VMEM((outers, 1, rows_dev), jnp.int32),
            pltpu.VMEM((members, outers, 1, rows_dev), jnp.int32),
            pltpu.VMEM((outers, rows_dev, cols), BF16),
            pltpu.VMEM((parts, slots, part_cols), BF16),
            pltpu.VMEM((parts, slots, part_cols), BF16),
            pltpu.VMEM((parts, rows, part_cols), BF16),
            pltpu.VMEM((cols, rows), BF16),
            pltpu.VMEM((cols, rows), F32),
            pltpu.VMEM((outers, rows_dev, cols), BF16),
            pltpu.VMEM((groups, height, codes), F32),
            *moving,
            *moving,
            *moving_sems * 4,
            dma((3,)),
            dma((parts,)),
            *[dma((outers,))] * 6,
            *[dma((members,))] * 2,
            *[dma((parts, members))] * 2,
        ],
        compiler_params=pltpu.CompilerParams(
            collective_id=0, has_side_effects=True, vmem_limit_bytes=52 * 2**20
        ),
    )(list_ids.reshape(1, rows_dev), vectors, coarse_centroids, codebook)
    return full, grad.reshape(codebook.shape).astype(F32)


def solution(mesh):
    return jax.shard_map(
        on_device,
        mesh=mesh,
        in_specs=(
            P(("outer", "member"), None),
            P(("outer", "member")),
            P("member", None),
            P("outer", None, None),
        ),
        out_specs=(P(("outer", "member"), None), P("outer", None, None)),
        check_vma=False,
    )
```

time: 237 us -> 74.7 us (0.32)
  waiting for transfers between devices: 114 us -> 0 us
  blocking collectives: 77.1 us -> 0 us
  Pallas kernels: 12.6 us -> 67.4 us
  between operations: 14.1 us -> 0.65 us
  starting transfers between devices: 7.1 us -> 0 us
  matrix products: 4.38 us -> 0 us
    all_gather x1 -> x0, blocking collectives: 69.4 us -> none  [on_device(): ids_all = lax.all_gather(list_ids, ('member', 'outer'), axis=0, tiled=False)]
    reduce_scatter x1 -> x0, waiting for transfers between devices: 60.4 us -> none  [reduce_member(): mine = lax.psum_scatter(flat, 'member', scatter_dimension=0, tiled=True)]
    pallas_call x1, Pallas kernels: 12.6 us -> 67.4 us  [on_device(): pl.pallas_call(functools.partial(step_kernel, scale, sub, capacity, plan)...]
    all_gather x1 -> x0, waiting for transfers between devices: 34.4 us -> none  [reduce_member(): lax.all_gather(mine, 'member', axis=0, tiled=True).reshape(partial.shape)]
    all_to_all x2 -> x0, waiting for transfers between devices: 18.8 us -> none  [the longest x1 13.5 us: on_device(): lax.all_to_all(sent, 'member', split_axis=0, concat_axis=0, tiled=True)]
    all_to_all x1 -> x0, blocking collectives: 7.67 us -> none  [on_device(): lax.all_to_all(full, 'outer', split_axis=0, concat_axis=1, tiled=True)]
    all_to_all x2 -> x0, starting transfers between devices: 7.02 us -> none  [the longest x1 3.57 us: on_device(): lax.all_to_all(sent, 'member', split_axis=0, concat_axis=0, tiled=True)]
    dot_general x4 -> x0, matrix products: 4.38 us -> none  [the longest x1 3.84 us: on_device(): sent = jnp.dot(onehot, table, preferred_element_type=BF16)]
  transfers between devices with their start and end apart: 4 -> 0, of which waited for: 4 -> 0; matrix products, arithmetic and copies ran while one was open for 1% -> 0% of each run, Pallas kernels for 0% -> 0%
where the time goes in v3:
time: 74.7 us; the launch traced here: 74.5 us
  Pallas kernels  67.4 us (90%)
  other arithmetic  4.13 us (6%)
  local copies, waits for them, and re-layouts  2.3 us (3%)
    pallas_call x1, Pallas kernels, on_device(): pl.pallas_call(functools.partial(step_kernel, scale, sub, capacity, plan)...  67.4 us
    convert_element_type x1, other arithmetic, on_device(): return (full, grad.reshape(codebook.shape).astype(F32))  4.13 us
    unnamed x5, local copies, waits for them, and re-layouts  2.3 us

profile of v3, /device:TPU:0, one launch (start us, length us, event | category | flops | bytes accessed | tf_op | source)
XLA Modules:
  0.0 74.5 jit_solution(2439983522289771528)
XLA Ops:
  0.6 0.0 copy-start
  0.6 0.9 %copy-done = bf16[128,1024]{1,0:T(8,128)(2,1)S(1)} copy-done((bf16[128,1024]{1,0:T(8,128)(2,1)S(1)}, bf16[128,1024]{1,0:T(8,128)(2,1)}, u32[]{:S(2)}) %copy-start) | copy-done | bytes 262168
  1.6 0.0 copy-start.1
  1.6 0.7 copy-done.1
  2.2 67.4 %shard_map.59 = (bf16[128,1024]{1,0:T(8,128)(2,1)S(1)}, bf16[8,64,2048]{2,1,0:T(8,128)(2,1)}) custom-call(s32[1,128]{1,0:T(1,128)S(1)} %bitcast.1, bf16[128,1024]{1,0:T(8,128)(2,1)S(1)} %copy-done, bf16[2048,1024]{1,0:T(8,128)(2,1)} %table_hbm.1, bf16[8,64,2048]{2,1,0:T(8,128)(2,1)} %code_hbm.1), custom_call_target="tpu_custom_call" | custom-call | tf_op jit(solution)/shard_map/pallas_call | solution.py:450
  69.7 4.1 %convert_element_type.3 = f32[8,64,2048]{2,1,0:T(8,128)} convert(bf16[8,64,2048]{2,1,0:T(8,128)(2,1)} %get-tuple-element.5) | non-fusion elementwise | flops 1048576 | bytes 6291456 | tf_op jit(solution)/shard_map/convert_element_type | solution.py:486
  73.8 0.7 copy.7
Async XLA Ops:
  0.6 1.0 %copy-start = (bf16[128,1024]{1,0:T(8,128)(2,1)S(1)}, bf16[128,1024]{1,0:T(8,128)(2,1)}, u32[]{:S(2)}) copy-start(bf16[128,1024]{1,0:T(8,128)(2,1)} %vec_hbm.1) | copy-start | bytes 786436
  1.6 0.7 copy-start.1

commit v4 on v3

--- a/solution.py
+++ b/solution.py
@@ -21,19 +21,22 @@
     return hi, mid, low
 
 
-def one_subspace(code, res_t, scale):
-    rows = res_t.shape[1]
-    codes = code.shape[1]
+def code_operand(code):
     code_wide = code.astype(F32)
     norm = (-0.5 * LOG2E) * jnp.sum(code_wide * code_wide, axis=0, keepdims=True)
     hi, mid, low = pieces(norm)
-    row_index = lax.broadcasted_iota(jnp.int32, (16, codes), 0)
+    row_index = lax.broadcasted_iota(jnp.int32, (16, code.shape[1]), 0)
     tail = jnp.where(
         row_index == 0,
         hi.astype(F32),
         jnp.where(row_index == 1, mid.astype(F32), jnp.where(row_index == 2, low.astype(F32), 0.0)),
     ).astype(BF16)
-    right = jnp.concatenate([code, code, code, tail], axis=0)
+    return jnp.concatenate([code, code, code, tail], axis=0)
+
+
+def one_subspace(code, right, res_t, scale):
+    rows = res_t.shape[1]
+    code_wide = code.astype(F32)
     ones = jnp.ones((16, rows), BF16)
     left = jnp.concatenate([*pieces(res_t.astype(F32) * LOG2E), ones], axis=0)
     logits = lax.dot_general(left, right, (((0,), (0,)), ((), ())), preferred_element_type=F32)
@@ -100,6 +103,7 @@
     reb_t,
     back,
     acc,
+    right_ref,
     *rest,
 ):
     stages = len(plan)
@@ -232,6 +236,12 @@
         place = picked(wanted) & (slot_outer == source)
         places.append(jnp.where(place, 1.0, 0.0).T.astype(BF16))
     place_all = jnp.concatenate(places, axis=0)
+    loads[2].wait()
+    spaces = code_ref.shape[0]
+
+    @pl.loop(0, spaces // 2)
+    def _(space):
+        right_ref[space] = code_operand(code_ref[space])
 
     @pl.loop(1, members)
     def _(step):
@@ -355,7 +365,7 @@
         lags.append(lag)
 
     def advance(tick):
-        for (take, stage), lag in reversed(list(zip(work, lags))):
+        for (take, stage), lag in zip(work, lags):
             group = tick - lag
 
             @pl.when((group >= 0) & (group < groups))
@@ -364,7 +374,11 @@
 
     for _, vec_copy in outer_pairs:
         vec_copy.wait()
-    loads[2].wait()
+
+    @pl.loop(spaces // 2, spaces)
+    def _(space):
+        right_ref[space] = code_operand(code_ref[space])
+
     part_groups = groups // parts
 
     @pl.loop(0, parts)
@@ -386,7 +400,9 @@
             for inner in range(per_group):
                 space = tick * per_group + inner
                 at = pl.ds(pl.multiple_of(space * sub, sub), sub)
-                rebuilt_t, grad = one_subspace(code_ref[space], res_t[at, :], scale)
+                rebuilt_t, grad = one_subspace(
+                    code_ref[space], right_ref[space], res_t[at, :], scale
+                )
                 reb_t[at, :] = rebuilt_t
                 acc[tick, inner * sub : (inner + 1) * sub, :] = grad
             advance(tick)
@@ -422,7 +438,7 @@
         back_copy(step).wait()
 
 
-PARTS = 2
+PARTS = 4
 
 
 def on_device(vectors, list_ids, coarse_centroids, codebook):
@@ -470,6 +486,7 @@
             pltpu.VMEM((cols, rows), F32),
             pltpu.VMEM((outers, rows_dev, cols), BF16),
             pltpu.VMEM((groups, height, codes), F32),
+            pltpu.VMEM((spaces, 3 * sub + 16, codes), BF16),
             *moving,
             *moving,
             *moving_sems * 4,
@@ -480,7 +497,7 @@
             *[dma((parts, members))] * 2,
         ],
         compiler_params=pltpu.CompilerParams(
-            collective_id=0, has_side_effects=True, vmem_limit_bytes=52 * 2**20
+            collective_id=0, has_side_effects=True, vmem_limit_bytes=60 * 2**20
         ),
     )(list_ids.reshape(1, rows_dev), vectors, coarse_centroids, codebook)
     return full, grad.reshape(codebook.shape).astype(F32)

time: 74.7 us -> 68.2 us (0.913)
  Pallas kernels: 67.4 us -> 62.5 us
  local copies, waits for them, and re-layouts: 2.3 us -> 0.71 us
    pallas_call x1, Pallas kernels: 67.4 us -> 62.5 us  [on_device(): pl.pallas_call(functools.partial(step_kernel, scale, sub, capacity, plan)...]
    unnamed x5 -> x3, local copies, waits for them, and re-layouts: 2.3 us -> 0.71 us
where the time goes in v4:
time: 68.2 us; the launch traced here: 68 us
  Pallas kernels  62.5 us (92%)
  other arithmetic  4.17 us (6%)
  local copies, waits for them, and re-layouts  0.71 us (1%)
    pallas_call x1, Pallas kernels, on_device(): pl.pallas_call(functools.partial(step_kernel, scale, sub, capacity, plan)...  62.5 us
    convert_element_type x1, other arithmetic, on_device(): return (full, grad.reshape(codebook.shape).astype(F32))  4.17 us

profile of v4, /device:TPU:0, one launch (start us, length us, event | category | flops | bytes accessed | tf_op | source)
XLA Modules:
  0.0 68.0 jit_solution(11056246695962140142)
XLA Ops:
  0.6 62.5 %shard_map.59 = (bf16[128,1024]{1,0:T(8,128)(2,1)}, bf16[8,64,2048]{2,1,0:T(8,128)(2,1)}) custom-call(s32[1,128]{1,0:T(1,128)} %bitcast.1, bf16[128,1024]{1,0:T(8,128)(2,1)} %vec_hbm.1, bf16[2048,1024]{1,0:T(8,128)(2,1)} %table_hbm.1, bf16[8,64,2048]{2,1,0:T(8,128)(2,1)} %code_hbm.1), custom_call_target="tpu_custom_call" | custom-call | tf_op jit(solution)/shard_map/pallas_call | solution.py:466
  63.2 0.0 copy-start
  63.2 4.2 %convert_element_type.3 = f32[8,64,2048]{2,1,0:T(8,128)} convert(bf16[8,64,2048]{2,1,0:T(8,128)(2,1)} %get-tuple-element.5) | non-fusion elementwise | flops 1048576 | bytes 6291456 | tf_op jit(solution)/shard_map/convert_element_type | solution.py:503
  67.3 0.0 copy-done
  67.3 0.7 %copy.7 = bf16[128,1024]{1,0:T(8,128)(2,1)} copy(bf16[128,1024]{1,0:T(8,128)(2,1)S(1)} %copy-done) | data formatting | bytes 524288
Async XLA Ops:
  63.2 4.2 %copy-start = (bf16[128,1024]{1,0:T(8,128)(2,1)S(1)}, bf16[128,1024]{1,0:T(8,128)(2,1)}, u32[]{:S(2)}) copy-start(bf16[128,1024]{1,0:T(8,128)(2,1)} %get-tuple-element.8) | copy-start | bytes 786436
